TPU v7x, 128 devices: a whole 4x4x4 slice. The times are simulated.
128 devices in a mesh: section: 4 (over z_lo, core), fsdp: 32 (over y, x, z_hi).
Axes of the slice: x: 4, y: 4, z: 4 (z_hi: 2, z_lo: 2; z = z_hi * 2 + z_lo), core: 2. Of those that a mesh axis runs over, the one named last changes fastest.
Arguments:
- fwd_in: bfloat16 [4, 512, 6144], P('section', 'fsdp'), may hold values from -6 to 6
- saved: bfloat16 [4, 512, 6144], P('section', 'fsdp'), may hold values from -6 to 6
- gain: float32 [4, 6144], P('section'), may hold values from 0.1 to 1.9
- w_in: bfloat16 [4, 6144, 12288], P('section', None, 'fsdp'), may hold values from -0.078125 to 0.078125
- w_out: bfloat16 [4, 12288, 6144], P('section', 'fsdp'), may hold values from -0.0546875 to 0.0546875
- cot_in: bfloat16 [4, 512, 6144], P('section', 'fsdp'), may hold values from -6 to 6
Outputs:
- fwd_arrive: bfloat16 [4, 512, 6144], P('section', 'fsdp')
- cot_arrive: bfloat16 [4, 512, 6144], P('section', 'fsdp')
- grad_in: bfloat16 [4, 6144, 12288], P('section', None, 'fsdp')
- grad_out: bfloat16 [4, 12288, 6144], P('section', 'fsdp')
All inputs are finite; a program needn't handle non-finite values.
Results may differ from a plain program's by a relative error of at most 0.015.
Values may be sent and summed in bfloat16 or wider, within the bound.
A program may use at most 192 MiB of HBM per device.

v0:
```python
import math

import jax
import jax.numpy as jnp
from jax import lax
from jax.sharding import PartitionSpec as P

epsilon = 1e-06


def passed_along(shard, axis, by):
    peers = lax.axis_size(axis)
    pairs = [(i, i + by) for i in range(peers) if 0 <= i + by < peers]
    return lax.ppermute(shard, axis, pairs)


def normalize(rows):
    values = rows.astype(jnp.float32)
    center = values - jnp.mean(values, axis=-1, keepdims=True)
    scale = lax.rsqrt(jnp.mean(center * center, axis=-1, keepdims=True) + epsilon)
    return (center * scale, scale)


def gelu_slope(pre):
    cdf = 0.5 * (1.0 + jax.scipy.special.erf(pre * (1.0 / math.sqrt(2.0))))
    return cdf + pre * jnp.exp(-0.5 * pre * pre) * (1.0 / math.sqrt(2.0 * math.pi))


def norm_back(unit, scale, gain_row, incoming):
    grad_unit = incoming * gain_row
    mean_one = jnp.mean(grad_unit, axis=-1, keepdims=True)
    mean_two = jnp.mean(grad_unit * unit, axis=-1, keepdims=True)
    return scale * (grad_unit - mean_one - unit * mean_two)


def contract_first(left, right):
    return lax.dot_general(
        left, right, (((0,), (0,)), ((), ())), preferred_element_type=jnp.float32
    )


def contract_last(left, right):
    return lax.dot_general(
        left, right, (((1,), (1,)), ((), ())), preferred_element_type=jnp.float32
    )


def per_device(fwd_in, saved, gain, w_in, w_out, cot_in):
    gain_row = gain[0]
    w_first = w_in[0]
    w_second = w_out[0]
    local = fwd_in.shape[1]
    offset = lax.axis_index("fsdp") * local
    saved_all = lax.all_gather(saved[0], "fsdp", axis=0, tiled=True)
    unit_a, scale_a = normalize(saved_all)
    normed_a = (unit_a * gain_row).astype(jnp.bfloat16)
    pre_a = jnp.dot(normed_a, w_first, preferred_element_type=jnp.float32)
    hidden_a = jax.nn.gelu(pre_a, approximate=False).astype(jnp.bfloat16)
    slope_a = gelu_slope(pre_a)
    moving, coming = (fwd_in[0], cot_in[0])
    unit, scale = normalize(moving)
    normed = (unit * gain_row).astype(jnp.bfloat16)
    hidden = jax.nn.gelu(
        jnp.dot(
            lax.all_gather(normed, "fsdp", axis=0, tiled=True),
            w_first,
            preferred_element_type=jnp.float32,
        ),
        approximate=False,
    ).astype(jnp.bfloat16)
    block = hidden
    total = lax.psum_scatter(
        jnp.dot(block, w_second, preferred_element_type=jnp.float32).astype(jnp.bfloat16),
        "fsdp",
        scatter_dimension=0,
        tiled=True,
    ).astype(jnp.float32)
    result = (moving.astype(jnp.float32) + total).astype(jnp.bfloat16)
    cot_all = lax.all_gather(coming, "fsdp", axis=0, tiled=True)
    grad_hidden = contract_last(cot_all, w_second)
    grad_pre = (grad_hidden * slope_a).astype(jnp.bfloat16)
    block = grad_pre
    grad_norm = lax.psum_scatter(
        contract_last(block, w_first).astype(jnp.bfloat16), "fsdp", scatter_dimension=0, tiled=True
    ).astype(jnp.float32)
    unit = lax.dynamic_slice_in_dim(unit_a, offset, local, 0)
    scale = lax.dynamic_slice_in_dim(scale_a, offset, local, 0)
    back = (coming.astype(jnp.float32) + norm_back(unit, scale, gain_row, grad_norm)).astype(
        jnp.bfloat16
    )
    back, cot_all, grad_pre = (back, cot_all, grad_pre)
    arrived = passed_along(result, "section", 1)
    returned = passed_along(back, "section", -1)
    grad_first = contract_first(normed_a, grad_pre).astype(jnp.bfloat16)
    grad_second = contract_first(hidden_a, cot_all).astype(jnp.bfloat16)
    return (arrived[None], returned[None], grad_first[None], grad_second[None])


def solution(mesh):
    return jax.shard_map(
        per_device,
        mesh=mesh,
        in_specs=(
            P("section", "fsdp", None),
            P("section", "fsdp", None),
            P("section", None),
            P("section", None, "fsdp"),
            P("section", "fsdp", None),
            P("section", "fsdp", None),
        ),
        out_specs=(
            P("section", "fsdp", None),
            P("section", "fsdp", None),
            P("section", None, "fsdp"),
            P("section", "fsdp", None),
        ),
        check_vma=False,
    )
```

profile of v0, /device:TPU:1, one launch (start us, length us, event | category | flops | bytes accessed | tf_op | source)
XLA Modules:
  0.0 807.0 jit_solution(12502420177116338543)
XLA Ops:
  7.2 0.0 all-gather.8.cloned.1.call-start
  7.2 0.7 all-gather.8.cloned.1.call-update
  7.9 0.0 all-gather.10.cloned.1.call-start
  7.9 0.0 copy-start.3
  8.0 0.7 all-gather.10.cloned.1.call-update
  8.6 0.0 reduce-scatter.5.cloned.1.call-start
  8.7 97.7 %all-gather.8.cloned.1.call-done = bf16[1,512,6144]{2,1,0:T(8,128)(2,1)} async-done(((bf16[1,16,6144]{2,1,0:T(8,128)(2,1)}), bf16[1,512,6144]{2,1,0:T(8,128)(2,1)}) %all-gather.8.cloned.1.call-update) | async-done | bytes 6291472 | tf_op jit(solution)/shard_map/all_gather | solution.py:54
  106.4 0.0 copy-start
  106.4 0.0 copy-start.4
  106.4 3.8 convert_reduce_fusion
  110.3 0.7 copy-done
  111.0 1.8 fusion.3
  112.8 0.0 copy-done.3
  112.8 0.0 copy-done.4
  112.8 3.6 fusion.12
  116.4 83.4 %all-gather.10.cloned.1.call-done = bf16[1,512,6144]{2,1,0:T(8,128)(2,1)} async-done(((bf16[1,16,6144]{2,1,0:T(8,128)(2,1)}), bf16[1,512,6144]{2,1,0:T(8,128)(2,1)}) %all-gather.10.cloned.1.call-update) | async-done | bytes 6291472 | tf_op jit(solution)/shard_map/all_gather | solution.py:79
  199.8 7.7 fusion.21
  207.5 0.0 copy-start.1
  207.5 7.9 convolution_convert_fusion
  215.4 0.0 reduce-scatter.5.cloned.1.call-update
  215.4 0.2 all-gather.6.cloned.1.call-start
  215.6 0.0 copy-done.1
  215.6 0.2 convert_reduce_fusion.1
  215.8 0.2 fusion.57
  216.1 0.1 dynamic-slice.3
  216.2 0.0 copy-start.2
  216.2 9.7 %fusion.1 = f32[512,6144]{1,0:T(8,128)} fusion(bf16[1,512,6144]{2,1,0:T(8,128)(2,1)} %all-gather.8.cloned.1.call-done, f32[512]{0:T(512)S(1)} %add_rsqrt_fusion, f32[512]{0:T(512)S(1)} %broadcast_multiply_fusion), kind=kLoop, calls=%fused_computation.3 | loop fusion | flops 9437184 | bytes 18878464 | tf_op jit(solution)/shard_map/mul | solution.py:21
  225.9 217.9 %reduce-scatter.5.cloned.1.call-done = bf16[16,6144]{1,0:T(8,128)(2,1)} async-done(((bf16[512,6144]{1,0:T(8,128)(2,1)}), bf16[16,6144]{1,0:T(8,128)(2,1)}) %reduce-scatter.5.cloned.1.call-update) | async-done | bytes 196624 | tf_op jit(solution)/shard_map/reduce_scatter | solution.py:83
  443.8 1.3 fusion.62
  445.0 0.0 copy-done.2
  445.1 2.0 fusion.61
  447.1 0.0 all-gather.6.cloned.1.call-update
  447.1 0.0 reduce-scatter.3.cloned.1.call-start
  447.1 91.6 %all-gather.6.cloned.1.call-done = bf16[512,6144]{1,0:T(8,128)(2,1)} async-done(((bf16[16,6144]{1,0:T(8,128)(2,1)}), bf16[512,6144]{1,0:T(8,128)(2,1)}) %all-gather.6.cloned.1.call-update) | async-done | bytes 6291472 | tf_op jit(solution)/shard_map/all_gather | solution.py:65
  538.7 9.1 %fusion.28 = bf16[512,384]{1,0:T(8,128)(2,1)S(1)} fusion(bf16[512,6144]{1,0:T(8,128)(2,1)} %all-gather.6.cloned.1.call-done, bf16[1,6144,384]{2,1,0:T(8,128)(2,1)} %param.9), kind=kOutput, calls=%fused_computation.30 | convolution fusion | flops 2428698624 | bytes 11403264 | tf_op jit(solution)/shard_map/dot_general | solution.py:64
  547.8 7.7 convolution_convert_fusion.1
  555.6 0.0 reduce-scatter.3.cloned.1.call-update
  555.6 9.2 %fusion.5 = bf16[1,384,6144]{2,1,0:T(8,128)(2,1)} fusion(bf16[1,512,6144]{2,1,0:T(8,128)(2,1)} %all-gather.10.cloned.1.call-done, f32[512,384]{1,0:T(8,128)S(1)} %fusion.12), kind=kOutput, calls=%fused_computation.12 | convolution fusion | flops 2431057920 | bytes 11796480 | tf_op jit(solution)/shard_map/dot_general | solution.py:37
  564.8 3.3 collective-permute-start.1
  568.1 215.7 %reduce-scatter.3.cloned.1.call-done = bf16[16,6144]{1,0:T(8,128)(2,1)} async-done(((bf16[512,6144]{1,0:T(8,128)(2,1)}), bf16[16,6144]{1,0:T(8,128)(2,1)}) %reduce-scatter.3.cloned.1.call-update) | async-done | bytes 196624 | tf_op jit(solution)/shard_map/reduce_scatter | solution.py:72
  783.8 1.0 fusion.60
  784.8 5.3 collective-permute-start
  790.1 9.0 %fusion.4 = bf16[1,6144,384]{2,1,0:T(8,128)(2,1)} fusion(bf16[512,384]{1,0:T(8,128)(2,1)S(1)} %fusion.21, f32[6144]{0:T(1024)S(1)} %bitcast.80, bf16[1,512,6144]{2,1,0:T(8,128)(2,1)} %all-gather.8.cloned.1.call-done, f32[512]{0:T(512)S(1)} %add_rsqrt_fusion, f32[512]{0:T(512)S(1)} %broadcast_multiply_fusion), kind=kOutput, calls=%fused_computation.11 | convolution fusion | flops 2434007040 | bytes 11431936 | tf_op jit(solution)/shard_map/dot_general | solution.py:37
  799.1 0.0 collective-permute-done.1
  799.1 0.0 collective-permute-done
  799.1 0.7 copy.12
  799.8 0.7 copy.13
  (5 shorter events, 0.0 us)
Async XLA Ops:
  7.2 99.3 %all-gather.8.cloned.1.call-start = ((), (), s32[]{:S(2)}) async-start(), calls=%async_computation.5 | async-start | bytes 6488064 | tf_op jit(solution)/shard_map/all_gather | solution.py:54
  7.9 191.9 %all-gather.10.cloned.1.call-start = ((), (), s32[]{:S(2)}) async-start(), calls=%async_computation.6 | async-start | bytes 6488064 | tf_op jit(solution)/shard_map/all_gather | solution.py:79
  7.9 104.9 %copy-start.3 = (f32[1,6144]{1,0:T(1,128)S(1)}, f32[1,6144]{1,0:T(1,128)}, u32[]{:S(2)}) copy-start(f32[1,6144]{1,0:T(1,128)} %param.8) | copy-start | bytes 73732
  8.6 435.1 %reduce-scatter.5.cloned.1.call-start = ((), (), s32[]{:S(2)}) async-start(), calls=%async_computation.4 | async-start | bytes 6488064 | tf_op jit(solution)/shard_map/reduce_scatter | solution.py:83
  106.4 4.6 copy-start
  106.4 6.4 copy-start.4
  207.5 8.2 %copy-start.1 = (bf16[1,16,6144]{2,1,0:T(8,128)(2,1)S(1)}, bf16[1,16,6144]{2,1,0:T(8,128)(2,1)}, u32[]{:S(2)}) copy-start(bf16[1,16,6144]{2,1,0:T(8,128)(2,1)} %param.6) | copy-start | bytes 589828
  215.4 323.3 %all-gather.6.cloned.1.call-start = ((), (), s32[]{:S(2)}) async-start(), calls=%async_computation.2 | async-start | bytes 6488064 | tf_op jit(solution)/shard_map/all_gather | solution.py:65
  216.2 228.9 %copy-start.2 = (bf16[1,16,6144]{2,1,0:T(8,128)(2,1)S(1)}, bf16[1,16,6144]{2,1,0:T(8,128)(2,1)}, u32[]{:S(2)}) copy-start(bf16[1,16,6144]{2,1,0:T(8,128)(2,1)} %param.11) | copy-start | bytes 589828
  447.1 336.7 %reduce-scatter.3.cloned.1.call-start = ((), (), s32[]{:S(2)}) async-start(), calls=%async_computation.3 | async-start | bytes 6488064 | tf_op jit(solution)/shard_map/reduce_scatter | solution.py:72
  564.8 234.3 %collective-permute-start.1 = (bf16[16,6144]{1,0:T(8,128)(2,1)S(1)}, bf16[16,6144]{1,0:T(8,128)(2,1)S(1)}, u32[]{:S(2)}, u32[]{:S(2)}) collective-permute-start(bf16[16,6144]{1,0:T(8,128)(2,1)S(1)} %get-tuple-element.6), channel_id=1, source_target_pairs={{32,0},{64,32},{96,64},{33,1},{65,33},{97,65},{34,2},{66,34},{98,6... | collective-permute-start | bytes 589832 | tf_op jit(solution)/shard_map/ppermute | solution.py:14
  784.8 14.3 %collective-permute-start = (bf16[16,6144]{1,0:T(8,128)(2,1)S(1)}, bf16[16,6144]{1,0:T(8,128)(2,1)S(1)}, u32[]{:S(2)}, u32[]{:S(2)}) collective-permute-start(bf16[16,6144]{1,0:T(8,128)(2,1)S(1)} %fusion.60), channel_id=1, source_target_pairs={{0,32},{32,64},{64,96},{1,33},{33,65},{65,97},{2,34},{34,66},{66,9... | collective-permute-start | bytes 589832 | tf_op jit(solution)/shard_map/ppermute | solution.py:14
Sparse Core Ops, SparseCore 0:
  11.0 95.3 all-gather.7
  109.5 90.2 all-gather.9
  215.5 228.1 reduce-scatter.4
  447.2 91.4 all-gather.5
  555.7 228.0 reduce-scatter.2
where the time goes:
time: 807 us
  waiting for transfers between devices  708 us (88%)
  matrix products  54.2 us (7%)
  other arithmetic  20 us (2%)
  between operations  13.9 us (2%)
  starting transfers between devices  8.95 us (1%)
    reduce_scatter x1, waiting for transfers between devices, per_device(): lax.psum_scatter(contract_last(block, w_first).astype(jnp.bfloat16), 'fsd...  218 us
    reduce_scatter x1, waiting for transfers between devices, per_device(): lax.psum_scatter(jnp.dot(block, w_second, preferred_element_type=jnp.floa...  216 us
    all_gather x1, waiting for transfers between devices, per_device(): saved_all = lax.all_gather(saved[0], 'fsdp', axis=0, tiled=True)  97.7 us
    all_gather x1, waiting for transfers between devices, per_device(): lax.all_gather(normed, 'fsdp', axis=0, tiled=True)  91.6 us
    all_gather x1, waiting for transfers between devices, per_device(): cot_all = lax.all_gather(coming, 'fsdp', axis=0, tiled=True)  83.4 us
    dot_general x2, matrix products, contract_first(): lax.dot_general(left, right, (((0,), (0,)), ((), ())), preferred_element_...  18.2 us
  transfers between devices with their start and end apart: 7, of which 5 were waited for; matrix products, arithmetic and copies ran while one was open for 5% of the time, Pallas kernels for 0%

commit v1 on v0

v1 whole, which is shorter than its diff:
```python
import math

import jax
import jax.numpy as jnp
from jax import lax
from jax.experimental import pallas as pl
from jax.experimental.pallas import tpu as pltpu
from jax.sharding import PartitionSpec as P

MESH = pl.DeviceIdType.MESH
epsilon = 1e-06
RING = 4
PAIR = 2
UNITS = 4
ALL = slice(None)
bf16 = jnp.bfloat16
f32 = jnp.float32


def normalize(rows):
    values = rows.astype(f32)
    center = values - jnp.mean(values, axis=-1, keepdims=True)
    scale = lax.rsqrt(jnp.mean(center * center, axis=-1, keepdims=True) + epsilon)
    return (center * scale, scale)


def gelu_cdf(pre):
    return 0.5 * (1.0 + lax.erf(pre * (1.0 / math.sqrt(2.0))))


def product(left, right, dims):
    return lax.dot_general(left, right, ((dims[:1], dims[1:]), ((), ())), preferred_element_type=f32)


class Copies:
    def __init__(self, send_sem, recv_sem):
        self.send_sem, self.recv_sem, self.slots, self.sent = send_sem, recv_sem, {}, {}

    def slot(self, key):
        return self.slots.setdefault(key, len(self.slots))

    def descriptor(self, key, src, dst, device):
        i = self.slot(key)
        return pltpu.make_async_remote_copy(
            src_ref=src, dst_ref=dst, send_sem=self.send_sem.at[i], recv_sem=self.recv_sem.at[i],
            device_id=device, device_id_type=MESH,
        )

    def send(self, key, src, dst, device):
        copy = self.descriptor(key, src, dst, device)
        copy.start()
        self.sent[key] = copy

    def arrived(self, key, region, device):
        self.descriptor(key, region, region, device).wait_recv()

    def drain(self, name=None):
        for key in [k for k in self.sent if name is None or k[0] == name]:
            self.sent.pop(key).wait_send()


def body(
    fwd, saved, cot, gain, w_in, w_out,
    result, back, grad_in, grad_out,
    w1, w2, g_saved, g_cot, g_fwd, p_back, t1, t2, t3, t4, t5,
    acc, slope, hid_a, gpre, hid, totals, stage1, stage2,
    send_sem, recv_sem, load_sem, out_sem,
):
    d = fwd.shape[1]
    half = d // 2
    tile = stage1.shape[1]
    tiles = d // tile
    section, f = lax.axis_index("section"), lax.axis_index("fsdp")
    y, x, z = f // (RING * PAIR), lax.rem(f // PAIR, RING), lax.rem(f, PAIR)
    other = 1 - z

    def device(yy, xx, zz):
        return (section, (yy * RING + xx) * PAIR + zz)

    def ring(i, by):
        return lax.rem(i + by + RING, RING)

    here = {"A": (x, y), "B": (y, x)}
    near = {
        ("A", 1, 1): device(y, ring(x, 1), z), ("A", 1, -1): device(y, ring(x, -1), z),
        ("A", 3, 1): device(ring(y, 1), x, z), ("A", 3, -1): device(ring(y, -1), x, z),
    }
    for by in (1, -1):
        near["B", 1, by], near["B", 3, by] = near["A", 3, by], near["A", 1, by]
    across = device(y, x, other)

    def place(p, i1, i3, zz, cols):
        return (i3, i1, zz, ALL, cols) if p == "A" else (i1, i3, zz, ALL, cols)

    base = {"A": 0, "B": half}
    copies = Copies(send_sem, recv_sem)

    loads = [
        pltpu.make_async_copy(w_in, w1, load_sem.at[0]),
        pltpu.make_async_copy(w_out, w2, load_sem.at[1]),
    ]
    for load in loads:
        load.start()

    barrier = pltpu.get_barrier_semaphore()
    neighbours = [near["A", 1, 1], near["A", 1, -1], near["A", 3, 1], near["A", 3, -1], across]
    for neighbour in neighbours:
        pl.semaphore_signal(barrier, inc=1, device_id=neighbour, device_id_type=MESH)

    gain_row = gain[...]
    g_saved[y, x, z] = (normalize(saved[...])[0] * gain_row).astype(bf16)
    g_cot[y, x, z] = cot[...]
    g_fwd[y, x, z] = (normalize(fwd[...])[0] * gain_row).astype(bf16)
    pl.semaphore_wait(barrier, len(neighbours))

    class Gather:
        def __init__(self, name, buf):
            self.name, self.buf = name, buf

        def send(self, p, key, where, to):
            ref = self.buf.at[where]
            copies.send((self.name, p) + key, ref, ref, to)

        def wait(self, p, key, where):
            copies.arrived((self.name, p) + key, self.buf.at[where], across)

        def cols(self, p, part=None):
            if part is None:
                return pl.ds(base[p], half)
            return pl.ds(base[p] + (half // 2 if part < 0 else 0), half // 2)

        def spread(self, p, j, where):
            self.send(p, ("z", j), where, across)
            for by in (1, -1):
                self.send(p, ("long", by, j), where, near[p, 3, by])

        def start(self):
            for p in "AB":
                i1, i3 = here[p]
                own = place(p, i1, i3, z, self.cols(p))
                for by in (1, -1):
                    self.send(p, ("short", by), own, near[p, 1, by])
            for p in "AB":
                i1, i3 = here[p]
                self.spread(p, 0, place(p, i1, i3, z, self.cols(p)))

        def short_one(self):
            for p in "AB":
                i1, i3 = here[p]
                for j, by in ((1, 1), (2, -1)):
                    where = place(p, ring(i1, -by), i3, z, self.cols(p))
                    self.wait(p, ("short", by), where)
                    part = place(p, ring(i1, -by), i3, z, self.cols(p, by))
                    self.send(p, ("short2", by), part, near[p, 1, by])
                    self.spread(p, j, where)

        def short_two(self):
            for p in "AB":
                i1, i3 = here[p]
                for by in (1, -1):
                    self.wait(p, ("short2", by), place(p, ring(i1, 2), i3, z, self.cols(p, by)))
                self.spread(p, 3, place(p, ring(i1, 2), i3, z, self.cols(p)))

        def paired(self):
            for p in "AB":
                i1, i3 = here[p]
                for j, by in ((0, 0), (1, -1), (2, 1), (3, 2)):
                    self.wait(p, ("z", j), place(p, ring(i1, by), i3, other, self.cols(p)))
                for by in (1, -1):
                    self.send(p, ("longz", by), place(p, ALL, i3, other, self.cols(p)), near[p, 3, by])

        def long_one(self):
            for p in "AB":
                i1, i3 = here[p]
                for by in (1, -1):
                    for j, off in ((0, 0), (1, -1), (2, 1), (3, 2)):
                        self.wait(p, ("long", by, j), place(p, ring(i1, off), ring(i3, -by), z, self.cols(p)))
                    part = place(p, ALL, ring(i3, -by), z, self.cols(p, by))
                    self.send(p, ("long2", by), part, near[p, 3, by])

        def longz_one(self):
            for p in "AB":
                i1, i3 = here[p]
                for by in (1, -1):
                    self.wait(p, ("longz", by), place(p, ALL, ring(i3, -by), other, self.cols(p)))
                    part = place(p, ALL, ring(i3, -by), other, self.cols(p, by))
                    self.send(p, ("longz2", by), part, near[p, 3, by])

        def finish(self):
            for p in "AB":
                i1, i3 = here[p]
                for by in (1, -1):
                    self.wait(p, ("long2", by), place(p, ALL, ring(i3, 2), z, self.cols(p, by)))
                    self.wait(p, ("longz2", by), place(p, ALL, ring(i3, 2), other, self.cols(p, by)))

    width = half // UNITS

    class Scatter:
        def __init__(self, name, buf, r):
            self.name, self.buf, self.r = name, buf, r

        def cols(self, p, u, part=None):
            if part is None:
                return pl.ds(base[p] + u * width, width)
            return pl.ds(base[p] + u * width + (width // 2 if part < 0 else 0), width // 2)

        def slot(self, p, u):
            return (self.r * UNITS + u) * 2 + "AB".index(p)

        def send(self, p, u, key, where, dst, to):
            copies.send((self.name, p, u) + key, self.buf.at[where], dst, to)

        def wait(self, p, u, key, dst):
            copies.arrived((self.name, p, u) + key, dst, across)

        def add(self, where, *terms):
            if len(terms) == 1:
                self.buf[where] = self.buf[where] + terms[0][...]
            else:
                total = self.buf[where].astype(f32)
                for term in terms:
                    total += term[...].astype(f32)
                self.buf[where] = total.astype(bf16)

        def first(self, u):
            for p in "AB":
                i1, i3 = here[p]
                for k, by in enumerate((1, -1)):
                    where = place(p, ALL, ring(i3, 2), ALL, self.cols(p, u, by))
                    self.send(p, u, ("1", by), where, t1.at[self.slot(p, u), k], near[p, 3, by])

        def second(self, u):
            for p in "AB":
                i1, i3 = here[p]
                for k, by in enumerate((1, -1)):
                    slot = t1.at[self.slot(p, u), k]
                    self.wait(p, u, ("1", by), slot)
                    self.add(place(p, ALL, ring(i3, by), ALL, self.cols(p, u, by)), slot)
                    where = place(p, ALL, ring(i3, by), ALL, self.cols(p, u))
                    self.send(p, u, ("2", by), where, t2.at[self.slot(p, u), k], near[p, 3, by])

        def third(self, u):
            for p in "AB":
                i1, i3 = here[p]
                slots = [t2.at[self.slot(p, u), k] for k in range(2)]
                for k, by in enumerate((1, -1)):
                    self.wait(p, u, ("2", by), slots[k])
                self.add(place(p, ALL, i3, ALL, self.cols(p, u)), *slots)
                where = place(p, ALL, i3, other, self.cols(p, u))
                self.send(p, u, ("3",), where, t3.at[self.slot(p, u)], across)

        def fourth(self, u):
            for p in "AB":
                i1, i3 = here[p]
                slot = t3.at[self.slot(p, u)]
                self.wait(p, u, ("3",), slot)
                self.add(place(p, ALL, i3, z, self.cols(p, u)), slot)
                for k, by in enumerate((1, -1)):
                    where = place(p, ring(i1, 2), i3, z, self.cols(p, u, by))
                    self.send(p, u, ("4", by), where, t4.at[self.slot(p, u), k], near[p, 1, by])

        def fifth(self, u):
            for p in "AB":
                i1, i3 = here[p]
                for k, by in enumerate((1, -1)):
                    slot = t4.at[self.slot(p, u), k]
                    self.wait(p, u, ("4", by), slot)
                    self.add(place(p, ring(i1, by), i3, z, self.cols(p, u, by)), slot)
                    where = place(p, ring(i1, by), i3, z, self.cols(p, u))
                    self.send(p, u, ("5", by), where, t5.at[self.slot(p, u), k], near[p, 1, by])

        def last(self, u):
            for p in "AB":
                i1, i3 = here[p]
                slots = [t5.at[self.slot(p, u), k] for k in range(2)]
                for k, by in enumerate((1, -1)):
                    self.wait(p, u, ("5", by), slots[k])
                total = self.buf[place(p, i1, i3, z, self.cols(p, u))].astype(f32)
                for slot in slots:
                    total += slot[...].astype(f32)
                totals[self.r, :, self.cols(p, u)] = total

    tokens = RING * RING * PAIR * fwd.shape[0]

    def gathered(buf, cols):
        return buf[:, :, :, :, cols].reshape(tokens, tile)

    def tile_cols(k):
        return pl.ds(pl.multiple_of(k * tile, tile), tile)

    def over_features(buf, weight, dims):
        acc[...] = jnp.zeros_like(acc)

        @pl.loop(0, tiles)
        def _(k):
            cols = tile_cols(k)
            rhs = weight[cols, :] if dims == (1, 0) else weight[:, cols]
            acc[...] += product(gathered(buf, cols), rhs, dims)

    def partial_sums(buf, left, weight, dims):
        @pl.loop(0, tiles)
        def _(k):
            cols = tile_cols(k)
            rhs = weight[:, cols] if dims == (1, 0) else weight[cols, :]
            buf[:, :, :, :, cols] = product(left[...], rhs, dims).astype(bf16).reshape(buf.shape[:4] + (tile,))

    def hidden_of(dst):
        pre = acc[...]
        dst[...] = (pre * gelu_cdf(pre)).astype(bf16)

    out_copies = {}

    def grads(k):
        cols = pl.ds(k * tile, tile)
        slot = k % 2
        for which, stage in ((0, stage1), (1, stage2)):
            if (which, slot) in out_copies:
                out_copies.pop((which, slot)).wait()
            if which == 0:
                stage[slot] = product(gathered(g_saved, cols), gpre[...], (0, 0)).astype(bf16)
                dst = grad_in.at[cols, :]
            else:
                stage[slot] = product(hid_a[...], gathered(g_cot, cols), (0, 0)).astype(bf16)
                dst = grad_out.at[:, cols]
            copy = pltpu.make_async_copy(stage.at[slot], dst, out_sem.at[which, slot])
            copy.start()
            out_copies[which, slot] = copy

    a, c, n = Gather("saved", g_saved), Gather("cot", g_cot), Gather("fwd", g_fwd)
    for g in (a, c, n):
        g.start()
    a.short_one()
    a.short_two()
    c.short_one()
    c.short_two()
    a.paired()
    c.paired()
    a.long_one()
    a.longz_one()
    n.short_one()
    n.short_two()
    c.long_one()
    c.longz_one()
    a.finish()
    loads[0].wait()
    over_features(g_saved, w1, (1, 0))
    pre = acc[...]
    cdf = gelu_cdf(pre)
    hid_a[...] = (pre * cdf).astype(bf16)
    slope[...] = cdf + pre * jnp.exp(-0.5 * pre * pre) * (1.0 / math.sqrt(2.0 * math.pi))
    n.paired()
    c.finish()
    loads[1].wait()
    over_features(g_cot, w2, (1, 1))
    gpre[...] = (acc[...] * slope[...]).astype(bf16)
    n.long_one()
    partial_sums(p_back, gpre, w1, (1, 1))
    rb, rf = Scatter("back", p_back, 0), Scatter("total", g_fwd, 1)
    for u in range(UNITS):
        rb.first(u)
    n.longz_one()
    rb.second(0)
    n.finish()
    over_features(g_fwd, w1, (1, 0))
    hidden_of(hid)
    rb.second(1)
    rb.third(0)
    copies.drain("fwd")
    partial_sums(g_fwd, hid, w2, (1, 0))
    for u in range(UNITS):
        rf.first(u)
    units = [(rb, u) for u in range(UNITS)] + [(rf, u) for u in range(UNITS)]
    done = {("second", 0), ("second", 1), ("third", 0)}
    todo = list(range(tiles))
    for t in range(1, len(units) + 4):
        for lag, stage in enumerate(("second", "third", "fourth", "fifth", "last")):
            i = t - lag
            if 0 <= i < len(units) and (stage, i) not in done:
                getattr(units[i][0], stage)(units[i][1])
        for k in todo[:2]:
            grads(k)
        todo = todo[2:]

    result[...] = (fwd[...].astype(f32) + totals[1]).astype(bf16)
    unit, scale = normalize(saved[...])
    grad_unit = totals[0] * gain_row
    mean_one = jnp.mean(grad_unit, axis=-1, keepdims=True)
    mean_two = jnp.mean(grad_unit * unit, axis=-1, keepdims=True)
    back[...] = (cot[...].astype(f32) + scale * (grad_unit - mean_one - unit * mean_two)).astype(bf16)
    copies.drain()
    for copy in out_copies.values():
        copy.wait()


def tick(fwd, saved, cot, gain, w_in, w_out):
    rows, d = fwd.shape
    ff = w_in.shape[1]
    tokens = rows * RING * RING * PAIR
    tile = min(512, d // 4)
    half = d // 2
    width = half // UNITS
    slots = 2 * UNITS * 2
    gathered = pltpu.VMEM((RING, RING, PAIR, rows, d), bf16)
    vmem = pl.BlockSpec(memory_space=pltpu.VMEM)
    hbm = pl.BlockSpec(memory_space=pl.ANY)
    n_copies = 3 * 2 * 22 + 2 * UNITS * 2 * 9
    return pl.pallas_call(
        body,
        out_shape=[
            jax.ShapeDtypeStruct((rows, d), bf16),
            jax.ShapeDtypeStruct((rows, d), bf16),
            jax.ShapeDtypeStruct((d, ff), bf16),
            jax.ShapeDtypeStruct((ff, d), bf16),
        ],
        in_specs=[vmem, vmem, vmem, vmem, hbm, hbm],
        out_specs=[vmem, vmem, hbm, hbm],
        scratch_shapes=[
            pltpu.VMEM((d, ff), bf16),
            pltpu.VMEM((ff, d), bf16),
            gathered, gathered, gathered, gathered,
            pltpu.VMEM((slots, 2, RING, PAIR, rows, width // 2), bf16),
            pltpu.VMEM((slots, 2, RING, PAIR, rows, width), bf16),
            pltpu.VMEM((slots, RING, rows, width), bf16),
            pltpu.VMEM((slots, 2, rows, width // 2), bf16),
            pltpu.VMEM((slots, 2, rows, width), bf16),
            pltpu.VMEM((tokens, ff), f32),
            pltpu.VMEM((tokens, ff), f32),
            pltpu.VMEM((tokens, ff), bf16),
            pltpu.VMEM((tokens, ff), bf16),
            pltpu.VMEM((tokens, ff), bf16),
            pltpu.VMEM((2, rows, d), f32),
            pltpu.VMEM((2, tile, ff), bf16),
            pltpu.VMEM((2, ff, tile), bf16),
            pltpu.SemaphoreType.DMA((n_copies,)),
            pltpu.SemaphoreType.DMA((n_copies,)),
            pltpu.SemaphoreType.DMA((2,)),
            pltpu.SemaphoreType.DMA((2, 2)),
        ],
        compiler_params=pltpu.CompilerParams(
            collective_id=0, has_side_effects=True, vmem_limit_bytes=62 * 2**20
        ),
        cost_estimate=pl.CostEstimate(
            flops=14 * tokens * d * ff, bytes_accessed=16 * d * ff, transcendentals=3 * tokens * ff
        ),
    )(fwd, saved, cot, gain, w_in, w_out)


def passed_along(shard, axis, by):
    peers = lax.axis_size(axis)
    pairs = [(i, i + by) for i in range(peers) if 0 <= i + by < peers]
    return lax.ppermute(shard, axis, pairs)


def per_device(fwd_in, saved, gain, w_in, w_out, cot_in):
    result, back, grad_first, grad_second = tick(
        fwd_in[0], saved[0], cot_in[0], gain, w_in[0], w_out[0]
    )
    arrived = passed_along(result, "section", 1)
    returned = passed_along(back, "section", -1)
    return (arrived[None], returned[None], grad_first[None], grad_second[None])


def solution(mesh):
    return jax.shard_map(
        per_device,
        mesh=mesh,
        in_specs=(
            P("section", "fsdp", None),
            P("section", "fsdp", None),
            P("section", None),
            P("section", None, "fsdp"),
            P("section", "fsdp", None),
            P("section", "fsdp", None),
        ),
        out_specs=(
            P("section", "fsdp", None),
            P("section", "fsdp", None),
            P("section", None, "fsdp"),
            P("section", "fsdp", None),
        ),
        check_vma=False,
    )
```

time: 807 us -> 199 us (0.25)
  waiting for transfers between devices: 708 us -> 5.27 us
  Pallas kernels: 0 us -> 172 us
  matrix products: 54.2 us -> 0 us
  other arithmetic: 20 us -> 0.01 us
  between operations: 13.9 us -> 0.66 us
    reduce_scatter x2 -> x0, waiting for transfers between devices: 434 us -> none  [the longest x1 218 us: per_device(): lax.psum_scatter(contract_last(block, w_first).astype(jnp.bfloat16), 'fsd...]
    all_gather x3 -> x0, waiting for transfers between devices: 273 us -> none  [the longest x1 97.7 us: per_device(): saved_all = lax.all_gather(saved[0], 'fsdp', axis=0, tiled=True)]
    pallas_call x0 -> x1, Pallas kernels: none -> 172 us  [tick(): pl.pallas_call(body, out_shape=[jax.ShapeDtypeStruct((rows, d), bf16), ja...]
    dot_general x7 -> x0, matrix products: 54.2 us -> none  [the longest x2 18.2 us: contract_first(): lax.dot_general(left, right, (((0,), (0,)), ((), ())), preferred_element_...]
    mul x1 -> x0, other arithmetic: 9.72 us -> none  [normalize(): return (center * scale, scale)]
  transfers between devices with their start and end apart: 7 -> 2, of which waited for: 5 -> 2; matrix products, arithmetic and copies ran while one was open for 5% -> 0% of each run, Pallas kernels for 0% -> 0%
where the time goes in v1:
time: 199 us
  Pallas kernels  172 us (86%)
  starting transfers between devices  12.6 us (6%)
  local copies, waits for them, and re-layouts  8.94 us (4%)
  waiting for transfers between devices  5.27 us (3%)
    pallas_call x1, Pallas kernels, tick(): pl.pallas_call(body, out_shape=[jax.ShapeDtypeStruct((rows, d), bf16), ja...  172 us
    ppermute x2, starting transfers between devices, passed_along(): return lax.ppermute(shard, axis, pairs)  12.6 us
    unnamed x8, local copies, waits for them, and re-layouts  8.94 us
    ppermute x2, waiting for transfers between devices, passed_along(): return lax.ppermute(shard, axis, pairs)  5.27 us
  transfers between devices with their start and end apart: 2, of which 2 were waited for; matrix products, arithmetic and copies ran while one was open for 0% of the time, Pallas kernels for 0%

profile of v1, /device:TPU:1, one launch (start us, length us, event | category | flops | bytes accessed | tf_op | source)
XLA Modules:
  0.0 199.2 jit_solution(15408259231964431674)
XLA Ops:
  0.6 171.6 %shard_map.93 = (bf16[16,6144]{1,0:T(8,128)(2,1)}, bf16[16,6144]{1,0:T(8,128)(2,1)}, bf16[6144,384]{1,0:T(8,128)(2,1)}, bf16[384,6144]{1,0:T(8,128)(2,1)}) custom-call(bf16[16,6144]{1,0:T(8,128)(2,1)} %bitcast.17, bf16[16,6144]{1,0:T(8,128)(2,1)} %bitcast.18, bf16[16,6144]{1,0:T(8,128)(2,1)} %bitcast.19, f32[1,6144]{1,0:T(1,128)} %gain.1, ...), custom_call_target="tpu_custom_call" | custom-call | flops 16911433728 | bytes 37748736 | tf_op jit(solution)/shard_map/pallas_call | solution.py:407
  172.3 10.7 %collective-permute-start = (bf16[16,6144]{1,0:T(8,128)(2,1)}, bf16[16,6144]{1,0:T(8,128)(2,1)S(1)}, u32[]{:S(2)}, u32[]{:S(2)}) collective-permute-start(bf16[16,6144]{1,0:T(8,128)(2,1)} %get-tuple-element.8), channel_id=1, source_target_pairs={{0,32},{32,64},{64,96},{1,33},{33,65},{65,97},{2,34},{34,66},{66,9... | collective-permute-start | bytes 589832 | tf_op jit(solution)/shard_map/ppermute | solution.py:451
  183.0 1.9 collective-permute-start.1
  184.9 1.0 collective-permute-done
  185.9 4.3 %collective-permute-done.1 = bf16[16,6144]{1,0:T(8,128)(2,1)S(1)} collective-permute-done((bf16[16,6144]{1,0:T(8,128)(2,1)}, bf16[16,6144]{1,0:T(8,128)(2,1)S(1)}, u32[]{:S(2)}, u32[]{:S(2)}) %collective-permute-start.1) | collective-permute-done | bytes 196640 | tf_op jit(solution)/shard_map/ppermute | solution.py:451
  190.2 0.7 copy.14
  190.9 0.0 slice-start
  190.9 0.7 copy.15
  191.6 0.0 slice-start.1
  191.6 5.4 %copy.16 = bf16[1,6144,384]{2,1,0:T(8,128)(2,1)} copy(bf16[1,6144,384]{2,1,0:T(8,128)(2,1)} %bitcast.12) | data formatting | bytes 9437184
  197.0 0.0 slice-done
  197.0 0.0 slice-done.1
  197.0 2.2 %copy.17 = bf16[1,384,6144]{2,1,0:T(8,128)(2,1)} copy(bf16[1,384,6144]{2,1,0:T(8,128)(2,1)S(1)} %bitcast.11) | data formatting | bytes 9437184
  (1 shorter events, 0.0 us)
Async XLA Ops:
  172.3 13.6 %collective-permute-start = (bf16[16,6144]{1,0:T(8,128)(2,1)}, bf16[16,6144]{1,0:T(8,128)(2,1)S(1)}, u32[]{:S(2)}, u32[]{:S(2)}) collective-permute-start(bf16[16,6144]{1,0:T(8,128)(2,1)} %get-tuple-element.8), channel_id=1, source_target_pairs={{0,32},{32,64},{64,96},{1,33},{33,65},{65,97},{2,34},{34,66},{66,9... | collective-permute-start | bytes 589832 | tf_op jit(solution)/shard_map/ppermute | solution.py:451
  183.0 7.2 %collective-permute-start.1 = (bf16[16,6144]{1,0:T(8,128)(2,1)}, bf16[16,6144]{1,0:T(8,128)(2,1)S(1)}, u32[]{:S(2)}, u32[]{:S(2)}) collective-permute-start(bf16[16,6144]{1,0:T(8,128)(2,1)} %get-tuple-element.9), channel_id=1, source_target_pairs={{32,0},{64,32},{96,64},{33,1},{65,33},{97,65},{34,2},{66,34},{98,6... | collective-permute-start | bytes 589832 | tf_op jit(solution)/shard_map/ppermute | solution.py:451
  190.9 6.1 %slice-start = ((s8[4718592]{0:T(1024)(128)(4,1)}), s8[4194304]{0:T(1024)(128)(4,1)S(1)}, s32[]{:S(2)}) async-start(s8[4718592]{0:T(1024)(128)(4,1)} %bitcast.9), calls=%async_computation | async-start | bytes 8388608
  191.6 5.4 %slice-start.1 = ((s8[4718592]{0:T(1024)(128)(4,1)}), s8[524288]{0:T(1024)(128)(4,1)S(1)}, s32[]{:S(2)}) async-start(s8[4718592]{0:T(1024)(128)(4,1)} %bitcast.9), calls=%async_computation.1 | async-start | bytes 1048576

commit v2 on v1

v2 whole, which is shorter than its diff:
```python
import math

import jax
import jax.numpy as jnp
from jax import lax
from jax.experimental import pallas as pl
from jax.experimental.pallas import tpu as pltpu
from jax.sharding import PartitionSpec as P

MESH = pl.DeviceIdType.MESH
epsilon = 1e-06
RING = 4
PAIR = 2
UNITS = 6
LATE = 512
CROSS = {"back": 0, "total": 1}
DIRECT = 3
LAGS = (0, 2, 4, 5, 6)
VMEM_MIB = 54
ALL = slice(None)
bf16 = jnp.bfloat16
f32 = jnp.float32


def normalize(rows):
    values = rows.astype(f32)
    center = values - jnp.mean(values, axis=-1, keepdims=True)
    scale = lax.rsqrt(jnp.mean(center * center, axis=-1, keepdims=True) + epsilon)
    return (center * scale, scale)


def gelu_cdf(pre):
    return 0.5 * (1.0 + lax.erf(pre * (1.0 / math.sqrt(2.0))))


def product(left, right, dims):
    return lax.dot_general(left, right, ((dims[:1], dims[1:]), ((), ())), preferred_element_type=f32)


class Copies:
    def __init__(self, send_sem, recv_sem):
        self.send_sem, self.recv_sem, self.slots, self.sent = send_sem, recv_sem, {}, {}

    def slot(self, key):
        return self.slots.setdefault(key, len(self.slots))

    def descriptor(self, key, src, dst, device):
        i = self.slot(key)
        return pltpu.make_async_remote_copy(
            src_ref=src, dst_ref=dst, send_sem=self.send_sem.at[i], recv_sem=self.recv_sem.at[i],
            device_id=device, device_id_type=MESH,
        )

    def send(self, key, src, dst, device):
        copy = self.descriptor(key, src, dst, device)
        copy.start()
        self.sent[key] = copy

    def arrived(self, key, region, device):
        self.descriptor(key, region, region, device).wait_recv()

    def drain(self, name=None):
        for key in [k for k in self.sent if name is None or k[0] == name]:
            self.sent.pop(key).wait_send()


def body(
    fwd, saved, cot, gain, w_in, w_out,
    fwd_arrive, cot_arrive, grad_in, grad_out,
    w1, w2, g_saved, g_cot, g_fwd, p_back, t0, t1, t2, t3, t4, t5,
    acc, slope, hid_a, gpre, hid, totals,
    result, back, result_in, back_in, fwd_in, last_in,
    send_sem, recv_sem, load_sem,
):
    d = fwd.shape[1]
    half = d // 2
    tile = half // UNITS
    tiles = d // tile
    section, f = lax.axis_index("section"), lax.axis_index("fsdp")
    y, x, z = f // (RING * PAIR), lax.rem(f // PAIR, RING), lax.rem(f, PAIR)
    other = 1 - z

    def device(yy, xx, zz):
        return (section, (yy * RING + xx) * PAIR + zz)

    def ring(i, by):
        return lax.rem(i + by + RING, RING)

    here = {"A": (x, y), "B": (y, x)}
    near = {
        ("A", 1, 1): device(y, ring(x, 1), z), ("A", 1, -1): device(y, ring(x, -1), z),
        ("A", 3, 1): device(ring(y, 1), x, z), ("A", 3, -1): device(ring(y, -1), x, z),
    }
    for by in (1, -1):
        near["B", 1, by], near["B", 3, by] = near["A", 3, by], near["A", 1, by]
    across = device(y, x, other)
    following = (ring(section, 1), f)
    next_at = {}
    for off in (0, 1, -1, 2):
        next_at["A", off] = (ring(section, 1), (y * RING + ring(x, off)) * PAIR + z)
        next_at["B", off] = (ring(section, 1), (ring(y, off) * RING + x) * PAIR + z)
    previous = (ring(section, -1), f)

    def place(p, i1, i3, zz, cols):
        return (i3, i1, zz, ALL, cols) if p == "A" else (i1, i3, zz, ALL, cols)

    base = {"A": 0, "B": half}
    width = half // UNITS
    copies = Copies(send_sem, recv_sem)

    loads = [
        pltpu.make_async_copy(w_in, w1, load_sem.at[0]),
        pltpu.make_async_copy(w_out, w2, load_sem.at[1]),
    ]
    for load in loads:
        load.start()

    barrier = pltpu.get_barrier_semaphore()
    neighbours = [near["A", 1, 1], near["A", 1, -1], near["A", 3, 1], near["A", 3, -1], across]
    neighbours += [following, previous]
    for by in (1, -1, 2):
        neighbours.append((ring(section, -1), (y * RING + ring(x, by)) * PAIR + z))
        neighbours.append((ring(section, -1), (ring(y, by) * RING + x) * PAIR + z))
    for neighbour in neighbours:
        pl.semaphore_signal(barrier, inc=1, device_id=neighbour, device_id_type=MESH)

    gain_row = gain[...]
    g_cot[y, x, z] = cot[...]
    pl.semaphore_wait(barrier, len(neighbours))

    class Gather:
        def __init__(self, name, buf):
            self.name, self.buf = name, buf

        def send(self, p, key, where, to):
            ref = self.buf.at[where]
            copies.send((self.name, p) + key, ref, ref, to)

        def wait(self, p, key, where):
            copies.arrived((self.name, p) + key, self.buf.at[where], across)

        def cols(self, p, part=None, span=half):
            if part is None:
                return pl.ds(base[p], span)
            return pl.ds(base[p] + (span // 2 if part < 0 else 0), span // 2)

        def early(self, p, part=None):
            return self.cols(p, part, half - LATE)

        def late(self, p):
            return pl.ds(base[p] + half - LATE, LATE)

        def spread(self, p, j, off):
            i1, i3 = here[p]
            self.send(p, ("z", j), place(p, ring(i1, off), i3, z, self.early(p)), across)
            where = place(p, ring(i1, off), i3, z, self.cols(p))
            for by in (1, -1):
                self.send(p, ("long", by, j), where, near[p, 3, by])

        def hand_over(self, p, j, off):
            if LATE == 0:
                return
            i1, i3 = here[p]
            self.send(p, ("late", j), place(p, ALL, ring(i3, off), z, self.late(p)), across)

        def start(self):
            for p in "AB":
                i1, i3 = here[p]
                own = place(p, i1, i3, z, self.cols(p))
                for by in (1, -1):
                    self.send(p, ("short", by), own, near[p, 1, by])
            for p in "AB":
                self.spread(p, 0, 0)

        def short_one(self):
            for p in "AB":
                i1, i3 = here[p]
                for j, by in ((1, 1), (2, -1)):
                    where = place(p, ring(i1, -by), i3, z, self.cols(p))
                    self.wait(p, ("short", by), where)
                    part = place(p, ring(i1, -by), i3, z, self.cols(p, by))
                    self.send(p, ("short2", by), part, near[p, 1, by])
                    self.spread(p, j, -by)

        def short_two(self):
            for p in "AB":
                i1, i3 = here[p]
                for by in (1, -1):
                    self.wait(p, ("short2", by), place(p, ring(i1, 2), i3, z, self.cols(p, by)))
                self.spread(p, 3, 2)
                self.hand_over(p, 0, 0)

        def paired(self):
            for p in "AB":
                i1, i3 = here[p]
                for j, by in ((0, 0), (1, -1), (2, 1), (3, 2)):
                    self.wait(p, ("z", j), place(p, ring(i1, by), i3, other, self.early(p)))
                for by in (1, -1):
                    self.send(p, ("longz", by), place(p, ALL, i3, other, self.early(p)), near[p, 3, by])

        def long_one(self):
            for p in "AB":
                i1, i3 = here[p]
                for by in (1, -1):
                    for j, off in ((0, 0), (1, -1), (2, 1), (3, 2)):
                        self.wait(p, ("long", by, j), place(p, ring(i1, off), ring(i3, -by), z, self.cols(p)))
                    part = place(p, ALL, ring(i3, -by), z, self.cols(p, by))
                    self.send(p, ("long2", by), part, near[p, 3, by])
                    self.hand_over(p, by, -by)

        def longz_one(self):
            for p in "AB":
                i1, i3 = here[p]
                for by in (1, -1):
                    self.wait(p, ("longz", by), place(p, ALL, ring(i3, -by), other, self.early(p)))
                    part = place(p, ALL, ring(i3, -by), other, self.early(p, by))
                    self.send(p, ("longz2", by), part, near[p, 3, by])

        def long_two(self):
            for p in "AB":
                i1, i3 = here[p]
                for by in (1, -1):
                    self.wait(p, ("long2", by), place(p, ALL, ring(i3, 2), z, self.cols(p, by)))
                self.hand_over(p, 2, 2)

        def longz_two(self):
            for p in "AB":
                i1, i3 = here[p]
                for by in (1, -1):
                    self.wait(p, ("longz2", by), place(p, ALL, ring(i3, 2), other, self.early(p, by)))

        def crossed(self):
            if LATE == 0:
                return
            for p in "AB":
                i1, i3 = here[p]
                for j, off in ((0, 0), (1, -1), (-1, 1), (2, 2)):
                    self.wait(p, ("late", j), place(p, ALL, ring(i3, off), other, self.late(p)))

    class Scatter:
        def __init__(self, name, buf, r):
            self.name, self.buf, self.r = name, buf, r
            self.cross = UNITS - CROSS[name]
            self.before = 0 if r == 0 else CROSS["back"]

        def crossing(self, p, u):
            return t0.at[self.before + u - self.cross, "AB".index(p)]

        def cols(self, p, u, part=None):
            if part is None:
                return pl.ds(base[p] + u * width, width)
            return pl.ds(base[p] + u * width + (width // 2 if part < 0 else 0), width // 2)

        def slot(self, p, u):
            return (self.r * UNITS + u) * 2 + "AB".index(p)

        def send(self, p, u, key, where, dst, to):
            copies.send((self.name, p, u) + key, self.buf.at[where], dst, to)

        def wait(self, p, u, key, dst):
            copies.arrived((self.name, p, u) + key, dst, across)

        def add(self, where, *terms):
            if len(terms) == 1:
                self.buf[where] = self.buf[where] + terms[0][...]
            else:
                total = self.buf[where].astype(f32)
                for term in terms:
                    total += term[...].astype(f32)
                self.buf[where] = total.astype(bf16)

        def depth(self, u):
            return z if u >= self.cross else ALL

        def landing(self, buf, p, u, k):
            return buf.at[self.slot(p, u), k, :, 0] if u >= self.cross else buf.at[self.slot(p, u), k]

        def zeroth(self):
            for u in range(self.cross, UNITS):
                for p in "AB":
                    where = place(p, ALL, ALL, other, self.cols(p, u))
                    self.send(p, u, ("0",), where, self.crossing(p, u), across)

        def first(self, u):
            for p in "AB":
                i1, i3 = here[p]
                if u >= self.cross:
                    slot = self.crossing(p, u)
                    self.wait(p, u, ("0",), slot)
                    self.add(place(p, ALL, ALL, z, self.cols(p, u)), slot)
                for k, by in enumerate((1, -1)):
                    where = place(p, ALL, ring(i3, 2), self.depth(u), self.cols(p, u, by))
                    self.send(p, u, ("1", by), where, self.landing(t1, p, u, k), near[p, 3, by])

        def second(self, u):
            for p in "AB":
                i1, i3 = here[p]
                for k, by in enumerate((1, -1)):
                    slot = self.landing(t1, p, u, k)
                    self.wait(p, u, ("1", by), slot)
                    self.add(place(p, ALL, ring(i3, by), self.depth(u), self.cols(p, u, by)), slot)
                    where = place(p, ALL, ring(i3, by), self.depth(u), self.cols(p, u))
                    self.send(p, u, ("2", by), where, self.landing(t2, p, u, k), near[p, 3, by])

        def third(self, u):
            for p in "AB":
                i1, i3 = here[p]
                slots = [self.landing(t2, p, u, k) for k in range(2)]
                for k, by in enumerate((1, -1)):
                    self.wait(p, u, ("2", by), slots[k])
                self.add(place(p, ALL, i3, self.depth(u), self.cols(p, u)), *slots)
                if u >= self.cross:
                    continue
                where = place(p, ALL, i3, other, self.cols(p, u))
                self.send(p, u, ("3",), where, t3.at[self.slot(p, u)], across)

        def fourth(self, u):
            for p in "AB":
                i1, i3 = here[p]
                if u < self.cross:
                    slot = t3.at[self.slot(p, u)]
                    self.wait(p, u, ("3",), slot)
                    self.add(place(p, ALL, i3, z, self.cols(p, u)), slot)
                if self.direct(u):
                    for k, off in enumerate((0, 1, -1, 2)):
                        where = place(p, ring(i1, off), i3, z, self.cols(p, u))
                        self.send(p, u, ("5", k), where, self.ending(p, u).at[k], next_at[p, off])
                    continue
                for k, by in enumerate((1, -1)):
                    where = place(p, ring(i1, 2), i3, z, self.cols(p, u, by))
                    self.send(p, u, ("4", by), where, t4.at[self.slot(p, u), k], near[p, 1, by])

        def direct(self, u):
            return self.name == "total" and u >= UNITS - DIRECT

        def ending(self, p, u):
            return last_in.at[u - (UNITS - DIRECT), "AB".index(p)]

        def fifth(self, u):
            if self.direct(u):
                return
            for p in "AB":
                i1, i3 = here[p]
                for k, by in enumerate((1, -1)):
                    slot = t4.at[self.slot(p, u), k]
                    self.wait(p, u, ("4", by), slot)
                    self.add(place(p, ring(i1, by), i3, z, self.cols(p, u, by)), slot)
                    where = place(p, ring(i1, by), i3, z, self.cols(p, u))
                    self.send(p, u, ("5", by), where, t5.at[self.slot(p, u), k], near[p, 1, by])

        def last(self, u):
            if self.direct(u):
                return
            for p in "AB":
                i1, i3 = here[p]
                slots = [t5.at[self.slot(p, u), k] for k in range(2)]
                for k, by in enumerate((1, -1)):
                    self.wait(p, u, ("5", by), slots[k])
                total = self.buf[place(p, i1, i3, z, self.cols(p, u))].astype(f32)
                for slot in slots:
                    total += slot[...].astype(f32)
                totals[self.r, :, self.cols(p, u)] = total

    tokens = RING * RING * PAIR * fwd.shape[0]

    def gathered(buf, cols):
        return buf[:, :, :, :, cols].reshape(tokens, tile)

    def tile_cols(k):
        return pl.ds(pl.multiple_of(k * tile, tile), tile)

    def over_features(buf, weight, dims, final):
        def term(k):
            cols = tile_cols(k)
            rhs = weight[cols, :] if dims == (1, 0) else weight[:, cols]
            return product(gathered(buf, cols), rhs, dims)

        if final:
            for k in (UNITS - 1, 2 * UNITS - 1):
                acc[...] += term(k)
            return
        acc[...] = term(0)

        @pl.loop(1, UNITS - 1)
        def _(k):
            acc[...] += term(k)

        @pl.loop(UNITS, 2 * UNITS - 1)
        def _(k):
            acc[...] += term(k)

    def partial_sums(buf, left, weight, dims, u):
        for p in "AB":
            cols = pl.ds(base[p] + u * width, width)
            rhs = weight[:, cols] if dims == (1, 0) else weight[cols, :]
            buf[:, :, :, :, cols] = product(left[...], rhs, dims).astype(bf16).reshape(buf.shape[:4] + (width,))

    def hidden_of(dst):
        pre = acc[...]
        dst[...] = (pre * gelu_cdf(pre)).astype(bf16)

    def grads(k):
        cols = pl.ds(k * tile, tile)
        grad_in[cols, :] = product(gathered(g_saved, cols), gpre[...], (0, 0)).astype(bf16)
        grad_out[:, cols] = product(hid_a[...], gathered(g_cot, cols), (0, 0)).astype(bf16)

    rest = DIRECT * width

    def send_result(hi):
        for p in "AB":
            cols = pl.ds(base[p], hi)
            result[:, cols] = (fwd[:, cols].astype(f32) + totals[1, :, cols]).astype(bf16)
            copies.send(("result", p), result.at[:, cols], result_in.at[:, cols], following)

    def rows_ahead(p):
        return pl.ds(base[p] + half - rest, rest), pl.ds("AB".index(p) * rest, rest)

    def send_rows():
        for p in "AB":
            mine, theirs = rows_ahead(p)
            copies.send(("rows", p), fwd.at[:, mine], fwd_in.at[:, theirs], following)

    def send_back():
        unit, scale = normalize(saved[...])
        grad_unit = totals[0] * gain_row
        mean_one = jnp.mean(grad_unit, axis=-1, keepdims=True)
        mean_two = jnp.mean(grad_unit * unit, axis=-1, keepdims=True)
        back[...] = (cot[...].astype(f32) + scale * (grad_unit - mean_one - unit * mean_two)).astype(bf16)
        copies.send(("back",), back, back_in, previous)

    a, c, n = Gather("saved", g_saved), Gather("cot", g_cot), Gather("fwd", g_fwd)
    c.start()
    g_saved[y, x, z] = (normalize(saved[...])[0] * gain_row).astype(bf16)
    a.start()
    g_fwd[y, x, z] = (normalize(fwd[...])[0] * gain_row).astype(bf16)
    n.start()
    send_rows()
    c.short_one()
    c.short_two()
    a.short_one()
    a.short_two()
    c.paired()
    a.paired()
    c.long_one()
    c.longz_one()
    a.long_one()
    a.longz_one()
    n.short_one()
    n.short_two()
    c.long_two()
    a.long_two()
    c.longz_two()
    loads[1].wait()
    over_features(g_cot, w2, (1, 1), False)
    n.paired()
    c.crossed()
    over_features(g_cot, w2, (1, 1), True)
    slope[...] = acc[...]
    a.longz_two()
    loads[0].wait()
    over_features(g_saved, w1, (1, 0), False)
    n.long_one()
    a.crossed()
    over_features(g_saved, w1, (1, 0), True)
    pre = acc[...]
    cdf = gelu_cdf(pre)
    hid_a[...] = (pre * cdf).astype(bf16)
    gelu_slope = cdf + pre * jnp.exp(-0.5 * pre * pre) * (1.0 / math.sqrt(2.0 * math.pi))
    gpre[...] = (slope[...] * gelu_slope).astype(bf16)

    rb, rf = Scatter("back", p_back, 0), Scatter("total", g_fwd, 1)
    units = [(rb, u) for u in range(UNITS)] + [(rf, u) for u in range(UNITS)]
    final = UNITS - 1

    done = set()

    def step(stage, i):
        if 0 <= i < len(units) and (stage, i) not in done:
            done.add((stage, i))
            r, u = units[i]
            getattr(r, stage)(u)

    def advance(t):
        for lag, stage in zip(LAGS, ("second", "third", "fourth", "fifth", "last")):
            step(stage, t - lag)

    def back_sums(u):
        partial_sums(p_back, gpre, w1, (1, 1), u)

    def total_sums(u):
        partial_sums(g_fwd, hid, w2, (1, 0), u)

    for u in range(rb.cross, UNITS):
        back_sums(u)
    rb.zeroth()
    for u in range(rb.cross):
        back_sums(u)
        rb.first(u)
        if u == 1:
            n.longz_one()
    n.long_two()
    advance(0)
    advance(1)
    n.longz_two()
    over_features(g_fwd, w1, (1, 0), False)
    advance(2)
    n.crossed()
    for u in range(rb.cross, UNITS):
        rb.first(u)
    over_features(g_fwd, w1, (1, 0), True)
    hidden_of(hid)
    advance(3)
    copies.drain("fwd")
    for u in range(rf.cross, UNITS):
        total_sums(u)
    rf.zeroth()
    advance(4)
    total_sums(0)
    rf.first(0)
    total_sums(1)
    rf.first(1)
    advance(5)
    for u in range(2, rf.cross):
        total_sums(u)
        rf.first(u)
    todo = list(range(tiles))
    for t in range(6, len(units) + LAGS[-1] + 1):
        if t == 2 * UNITS + 1:
            for i in (len(units) - 2, len(units) - 1):
                step("third", i)
                step("fourth", i)
        advance(t)
        if t == UNITS + 1:
            for u in range(rf.cross, UNITS):
                rf.first(u)
            copies.drain("cot")
            copies.drain("saved")
        if t == UNITS + LAGS[-1]:
            send_back()
        if t == 2 * UNITS - DIRECT - 1 + LAGS[-1]:
            send_result(half - DIRECT * width)
            copies.drain("back")
        for k in todo[:2]:
            grads(k)
        todo = todo[2:]

    copies.arrived(("back",), back_in, previous)
    cot_arrive[...] = jnp.where(section < lax.axis_size("section") - 1, back_in[...], jnp.zeros_like(back_in[...]))
    for p in "AB":
        cols = pl.ds(base[p], half - rest)
        copies.arrived(("result", p), result_in.at[:, cols], following)
        values = result_in[:, cols]
        fwd_arrive[:, cols] = jnp.where(section > 0, values, jnp.zeros_like(values))
        copies.arrived(("rows", p), fwd_in.at[:, rows_ahead(p)[1]], following)
    for u in range(UNITS - DIRECT, UNITS):
        for i, p in enumerate("AB"):
            here_in = rf.ending(p, u)
            for k in range(RING):
                copies.arrived(("total", p, u, "5", k), here_in.at[k], following)
            lo = i * rest + (u - (UNITS - DIRECT)) * width
            total = here_in[0].astype(f32)
            for k in range(1, RING):
                total += here_in[k].astype(f32)
            values = (fwd_in[:, pl.ds(lo, width)].astype(f32) + total).astype(bf16)
            fwd_arrive[:, rf.cols(p, u)] = jnp.where(section > 0, values, jnp.zeros_like(values))
    copies.drain()


def tick(fwd, saved, cot, gain, w_in, w_out):
    rows, d = fwd.shape
    ff = w_in.shape[1]
    tokens = rows * RING * RING * PAIR
    half = d // 2
    width = half // UNITS
    slots = 2 * UNITS * 2
    gathered = pltpu.VMEM((RING, RING, PAIR, rows, d), bf16)
    vmem = pl.BlockSpec(memory_space=pltpu.VMEM)
    hbm = pl.BlockSpec(memory_space=pl.ANY)
    n_copies = 3 * 2 * 26 + 2 * UNITS * 2 * 9 + 5
    return pl.pallas_call(
        body,
        out_shape=[
            pltpu.VMEM((rows, d), bf16),
            pltpu.VMEM((rows, d), bf16),
            pltpu.VMEM((d, ff), bf16),
            pltpu.VMEM((ff, d), bf16),
        ],
        in_specs=[vmem, vmem, vmem, vmem, hbm, hbm],
        out_specs=[vmem] * 4,
        scratch_shapes=[
            pltpu.VMEM((d, ff), bf16),
            pltpu.VMEM((ff, d), bf16),
            gathered, gathered, gathered, gathered,
            pltpu.VMEM((sum(CROSS.values()), 2, RING, RING, rows, width), bf16),
            pltpu.VMEM((slots, 2, RING, PAIR, rows, width // 2), bf16),
            pltpu.VMEM((slots, 2, RING, PAIR, rows, width), bf16),
            pltpu.VMEM((slots, RING, rows, width), bf16),
            pltpu.VMEM((slots, 2, rows, width // 2), bf16),
            pltpu.VMEM((slots, 2, rows, width), bf16),
            pltpu.VMEM((tokens, ff), f32),
            pltpu.VMEM((tokens, ff), f32),
            pltpu.VMEM((tokens, ff), bf16),
            pltpu.VMEM((tokens, ff), bf16),
            pltpu.VMEM((tokens, ff), bf16),
            pltpu.VMEM((2, rows, d), f32),
            *[pltpu.VMEM((rows, d), bf16)] * 4,
            pltpu.VMEM((rows, 2 * DIRECT * width), bf16),
            pltpu.VMEM((DIRECT, 2, RING, rows, width), bf16),
            pltpu.SemaphoreType.DMA((n_copies,)),
            pltpu.SemaphoreType.DMA((n_copies,)),
            pltpu.SemaphoreType.DMA((2,)),
        ],
        compiler_params=pltpu.CompilerParams(
            collective_id=0, has_side_effects=True, vmem_limit_bytes=VMEM_MIB * 2**20
        ),
        cost_estimate=pl.CostEstimate(
            flops=14 * tokens * d * ff, bytes_accessed=16 * d * ff, transcendentals=3 * tokens * ff
        ),
    )(fwd, saved, cot, gain, w_in, w_out)


def per_device(fwd_in, saved, gain, w_in, w_out, cot_in):
    outs = tick(fwd_in[0], saved[0], cot_in[0], gain, w_in[0], w_out[0])
    return tuple(out[None] for out in outs)


def solution(mesh):
    return jax.shard_map(
        per_device,
        mesh=mesh,
        in_specs=(
            P("section", "fsdp", None),
            P("section", "fsdp", None),
            P("section", None),
            P("section", None, "fsdp"),
            P("section", "fsdp", None),
            P("section", "fsdp", None),
        ),
        out_specs=(
            P("section", "fsdp", None),
            P("section", "fsdp", None),
            P("section", None, "fsdp"),
            P("section", "fsdp", None),
        ),
        check_vma=False,
    )
```

time: 199 us -> 181 us (0.910)
  starting transfers between devices: 12.6 us -> 0 us
  waiting for transfers between devices: 5.27 us -> 0 us
  local copies, waits for them, and re-layouts: 8.94 us -> 5.73 us
  Pallas kernels: 172 us -> 174 us
    ppermute x2 -> x0, starting transfers between devices: 12.6 us -> none  [passed_along(): return lax.ppermute(shard, axis, pairs)]
    ppermute x2 -> x0, waiting for transfers between devices: 5.27 us -> none  [passed_along(): return lax.ppermute(shard, axis, pairs)]
    unnamed x8 -> x4, local copies, waits for them, and re-layouts: 8.94 us -> 5.73 us
    pallas_call x1, Pallas kernels: 172 us -> 174 us  [tick(): pl.pallas_call(body, out_shape=[pltpu.VMEM((rows, d), bf16), pltpu.VMEM((...]
  transfers between devices with their start and end apart: 2 -> 0, of which waited for: 2 -> 0; matrix products, arithmetic and copies ran while one was open for 0% -> 0% of each run, Pallas kernels for 0% -> 0%
where the time goes in v2:
time: 181 us; the launch traced here: 180 us
  Pallas kernels  174 us (96%)
  local copies, waits for them, and re-layouts  5.73 us (3%)
    pallas_call x1, Pallas kernels, tick(): pl.pallas_call(body, out_shape=[pltpu.VMEM((rows, d), bf16), pltpu.VMEM((...  174 us
    unnamed x4, local copies, waits for them, and re-layouts  5.73 us

profile of v2, /device:TPU:1, one launch (start us, length us, event | category | flops | bytes accessed | tf_op | source)
XLA Modules:
  0.0 180.3 jit_solution(2150777660585995645)
XLA Ops:
  0.6 174.0 %shard_map.93 = (bf16[16,6144]{1,0:T(8,128)(2,1)S(1)}, bf16[16,6144]{1,0:T(8,128)(2,1)S(1)}, bf16[6144,384]{1,0:T(8,128)(2,1)S(1)}, bf16[384,6144]{1,0:T(8,128)(2,1)S(1)}) custom-call(bf16[16,6144]{1,0:T(8,128)(2,1)} %bitcast.15, bf16[16,6144]{1,0:T(8,128)(2,1)} %bitcast.16, bf16[16,6144]{1,0:T(8,128)(2,1)} %bitcast.17, f32[1,6144]{1,0:T(1,128)} %gain.1, ...), custom_call_target="tpu_custom_call" | custom-call | flops 16911433728 | bytes 37748736 | tf_op jit(solution)/shard_map/pallas_call | solution.py:580
  174.6 0.7 copy.14
  175.3 0.7 copy.15
  176.0 2.2 %copy.16 = bf16[1,6144,384]{2,1,0:T(8,128)(2,1)} copy(bf16[1,6144,384]{2,1,0:T(8,128)(2,1)S(1)} %bitcast.10) | data formatting | bytes 9437184
  178.2 2.2 %copy.17 = bf16[1,384,6144]{2,1,0:T(8,128)(2,1)} copy(bf16[1,384,6144]{2,1,0:T(8,128)(2,1)S(1)} %bitcast.9) | data formatting | bytes 9437184

commit v3 on v2

--- a/solution.py
+++ b/solution.py
@@ -14,8 +14,9 @@
 UNITS = 6
 LATE = 512
 CROSS = {"back": 0, "total": 1}
-DIRECT = 3
+DIRECT = 1
 LAGS = (0, 2, 4, 5, 6)
+TILES_A_STEP = 2
 VMEM_MIB = 54
 ALL = slice(None)
 bf16 = jnp.bfloat16
@@ -65,14 +66,14 @@
 
 
 def body(
-    fwd, saved, cot, gain, w_in, w_out,
+    fwd_rows, saved_rows, cot_rows, gain, w_in, w_out,
     fwd_arrive, cot_arrive, grad_in, grad_out,
     w1, w2, g_saved, g_cot, g_fwd, p_back, t0, t1, t2, t3, t4, t5,
     acc, slope, hid_a, gpre, hid, totals,
-    result, back, result_in, back_in, fwd_in, last_in,
+    fwd, saved, cot, result, back, result_in, back_in, fwd_in, last_in,
     send_sem, recv_sem, load_sem,
 ):
-    d = fwd.shape[1]
+    d = fwd_rows.shape[1]
     half = d // 2
     tile = half // UNITS
     tiles = d // tile
@@ -108,13 +109,6 @@
     width = half // UNITS
     copies = Copies(send_sem, recv_sem)
 
-    loads = [
-        pltpu.make_async_copy(w_in, w1, load_sem.at[0]),
-        pltpu.make_async_copy(w_out, w2, load_sem.at[1]),
-    ]
-    for load in loads:
-        load.start()
-
     barrier = pltpu.get_barrier_semaphore()
     neighbours = [near["A", 1, 1], near["A", 1, -1], near["A", 3, 1], near["A", 3, -1], across]
     neighbours += [following, previous]
@@ -124,8 +118,18 @@
     for neighbour in neighbours:
         pl.semaphore_signal(barrier, inc=1, device_id=neighbour, device_id_type=MESH)
 
+    own = (y, x, z)
+    loads = [
+        pltpu.make_async_copy(source, target, load_sem.at[i])
+        for i, (source, target) in enumerate(
+            ((w_in, w1), (w_out, w2), (cot_rows, g_cot.at[own]), (saved_rows, saved), (fwd_rows, fwd), (cot_rows, cot))
+        )
+    ]
+    for i in (2, 3, 4, 5, 1, 0):
+        loads[i].start()
+
     gain_row = gain[...]
-    g_cot[y, x, z] = cot[...]
+    loads[2].wait()
     pl.semaphore_wait(barrier, len(neighbours))
 
     class Gather:
@@ -430,11 +434,14 @@
 
     a, c, n = Gather("saved", g_saved), Gather("cot", g_cot), Gather("fwd", g_fwd)
     c.start()
+    loads[3].wait()
     g_saved[y, x, z] = (normalize(saved[...])[0] * gain_row).astype(bf16)
     a.start()
+    loads[4].wait()
     g_fwd[y, x, z] = (normalize(fwd[...])[0] * gain_row).astype(bf16)
     n.start()
     send_rows()
+    loads[5].wait()
     c.short_one()
     c.short_two()
     a.short_one()
@@ -514,25 +521,24 @@
     for u in range(rf.cross, UNITS):
         total_sums(u)
     rf.zeroth()
-    advance(4)
-    total_sums(0)
-    rf.first(0)
-    total_sums(1)
-    rf.first(1)
-    advance(5)
-    for u in range(2, rf.cross):
+    for t in range(4, UNITS):
+        advance(t)
+        total_sums(t - 4)
+        rf.first(t - 4)
+    for u in range(UNITS - 4, rf.cross):
         total_sums(u)
         rf.first(u)
     todo = list(range(tiles))
-    for t in range(6, len(units) + LAGS[-1] + 1):
+    for t in range(UNITS, len(units) + LAGS[-1] + 1):
         if t == 2 * UNITS + 1:
             for i in (len(units) - 2, len(units) - 1):
                 step("third", i)
                 step("fourth", i)
         advance(t)
-        if t == UNITS + 1:
+        if t == 2 * UNITS - 3:
             for u in range(rf.cross, UNITS):
                 rf.first(u)
+        if t == UNITS + 1:
             copies.drain("cot")
             copies.drain("saved")
         if t == UNITS + LAGS[-1]:
@@ -540,10 +546,11 @@
         if t == 2 * UNITS - DIRECT - 1 + LAGS[-1]:
             send_result(half - DIRECT * width)
             copies.drain("back")
-        for k in todo[:2]:
+        for k in todo[:TILES_A_STEP]:
             grads(k)
-        todo = todo[2:]
-
+        todo = todo[TILES_A_STEP:]
+
+    copies.drain()
     copies.arrived(("back",), back_in, previous)
     cot_arrive[...] = jnp.where(section < lax.axis_size("section") - 1, back_in[...], jnp.zeros_like(back_in[...]))
     for p in "AB":
@@ -563,7 +570,6 @@
                 total += here_in[k].astype(f32)
             values = (fwd_in[:, pl.ds(lo, width)].astype(f32) + total).astype(bf16)
             fwd_arrive[:, rf.cols(p, u)] = jnp.where(section > 0, values, jnp.zeros_like(values))
-    copies.drain()
 
 
 def tick(fwd, saved, cot, gain, w_in, w_out):
@@ -585,7 +591,7 @@
             pltpu.VMEM((d, ff), bf16),
             pltpu.VMEM((ff, d), bf16),
         ],
-        in_specs=[vmem, vmem, vmem, vmem, hbm, hbm],
+        in_specs=[hbm, hbm, hbm, vmem, hbm, hbm],
         out_specs=[vmem] * 4,
         scratch_shapes=[
             pltpu.VMEM((d, ff), bf16),
@@ -603,12 +609,12 @@
             pltpu.VMEM((tokens, ff), bf16),
             pltpu.VMEM((tokens, ff), bf16),
             pltpu.VMEM((2, rows, d), f32),
-            *[pltpu.VMEM((rows, d), bf16)] * 4,
+            *[pltpu.VMEM((rows, d), bf16)] * 7,
             pltpu.VMEM((rows, 2 * DIRECT * width), bf16),
             pltpu.VMEM((DIRECT, 2, RING, rows, width), bf16),
             pltpu.SemaphoreType.DMA((n_copies,)),
             pltpu.SemaphoreType.DMA((n_copies,)),
-            pltpu.SemaphoreType.DMA((2,)),
+            pltpu.SemaphoreType.DMA((6,)),
         ],
         compiler_params=pltpu.CompilerParams(
             collective_id=0, has_side_effects=True, vmem_limit_bytes=VMEM_MIB * 2**20
@@ -619,9 +625,30 @@
     )(fwd, saved, cot, gain, w_in, w_out)
 
 
+def move(*refs):
+    sources, targets, sem = refs[:4], refs[4:8], refs[8]
+    copies = [pltpu.make_async_copy(s, t, sem.at[i]) for i, (s, t) in enumerate(zip(sources, targets))]
+    for copy in copies:
+        copy.start()
+    for copy in copies:
+        copy.wait()
+
+
+def placed(*arrays):
+    hbm = pl.BlockSpec(memory_space=pl.ANY)
+    return pl.pallas_call(
+        move,
+        out_shape=[pltpu.HBM(a.shape, a.dtype) for a in arrays],
+        in_specs=[hbm] * 4,
+        out_specs=[hbm] * 4,
+        scratch_shapes=[pltpu.SemaphoreType.DMA((4,))],
+        compiler_params=pltpu.CompilerParams(vmem_limit_bytes=2 * 2**20),
+    )(*arrays)
+
+
 def per_device(fwd_in, saved, gain, w_in, w_out, cot_in):
     outs = tick(fwd_in[0], saved[0], cot_in[0], gain, w_in[0], w_out[0])
-    return tuple(out[None] for out in outs)
+    return tuple(out[None] for out in placed(*outs))
 
 
 def solution(mesh):

time: 181 us -> 178 us (0.983)
  local copies, waits for them, and re-layouts: 5.73 us -> 0 us
  Pallas kernels: 174 us -> 177 us
    unnamed x4 -> x0, local copies, waits for them, and re-layouts: 5.73 us -> none
    pallas_call x0 -> x1, Pallas kernels: none -> 3.91 us  [placed(): pl.pallas_call(move, out_shape=[pltpu.HBM(a.shape, a.dtype) for a in arra...]
where the time goes in v3:
time: 178 us
  Pallas kernels  177 us (99%)
    pallas_call x1, Pallas kernels, tick(): pl.pallas_call(body, out_shape=[pltpu.VMEM((rows, d), bf16), pltpu.VMEM((...  173 us
    pallas_call x1, Pallas kernels, placed(): pl.pallas_call(move, out_shape=[pltpu.HBM(a.shape, a.dtype) for a in arra...  3.91 us

profile of v3, /device:TPU:1, one launch (start us, length us, event | category | flops | bytes accessed | tf_op | source)
XLA Modules:
  0.0 178.0 jit_solution(16099505701688292825)
XLA Ops:
  0.6 173.3 %shard_map.93 = (bf16[16,6144]{1,0:T(8,128)(2,1)S(1)}, bf16[16,6144]{1,0:T(8,128)(2,1)S(1)}, bf16[6144,384]{1,0:T(8,128)(2,1)S(1)}, bf16[384,6144]{1,0:T(8,128)(2,1)S(1)}) custom-call(bf16[16,6144]{1,0:T(8,128)(2,1)} %bitcast.13, bf16[16,6144]{1,0:T(8,128)(2,1)} %bitcast.14, bf16[16,6144]{1,0:T(8,128)(2,1)} %bitcast.15, f32[1,6144]{1,0:T(1,128)} %gain.1, ...), custom_call_target="tpu_custom_call" | custom-call | flops 16911433728 | bytes 37748736 | tf_op jit(solution)/shard_map/pallas_call | solution.py:586
  173.9 3.9 %shard_map.94 = (bf16[16,6144]{1,0:T(8,128)(2,1)}, bf16[16,6144]{1,0:T(8,128)(2,1)}, bf16[6144,384]{1,0:T(8,128)(2,1)}, bf16[384,6144]{1,0:T(8,128)(2,1)}) custom-call(bf16[16,6144]{1,0:T(8,128)(2,1)S(1)} %get-tuple-element.12.refs_0_, bf16[16,6144]{1,0:T(8,128)(2,1)S(1)} %get-tuple-element.13.refs_1_, bf16[6144,384]{1,0:T(8,128)(2,1)S(1)} %get-tuple-element.14.refs_2_, ...), custom_call_target="tpu_custom_call" | custom-call | tf_op jit(solution)/shard_map/pallas_call | solution.py:639

commit v4 on v3

--- a/solution.py
+++ b/solution.py
@@ -16,7 +16,6 @@
 CROSS = {"back": 0, "total": 1}
 DIRECT = 1
 LAGS = (0, 2, 4, 5, 6)
-TILES_A_STEP = 2
 VMEM_MIB = 54
 ALL = slice(None)
 bf16 = jnp.bfloat16
@@ -506,11 +505,20 @@
         if u == 1:
             n.longz_one()
     n.long_two()
+    todo = list(range(tiles))
+
+    def some_grads(count):
+        for _ in range(min(count, len(todo))):
+            grads(todo.pop(0))
+
     advance(0)
+    some_grads(2)
     advance(1)
+    some_grads(1)
     n.longz_two()
     over_features(g_fwd, w1, (1, 0), False)
     advance(2)
+    some_grads(1)
     n.crossed()
     for u in range(rb.cross, UNITS):
         rb.first(u)
@@ -528,7 +536,6 @@
     for u in range(UNITS - 4, rf.cross):
         total_sums(u)
         rf.first(u)
-    todo = list(range(tiles))
     for t in range(UNITS, len(units) + LAGS[-1] + 1):
         if t == 2 * UNITS + 1:
             for i in (len(units) - 2, len(units) - 1):
@@ -546,9 +553,7 @@
         if t == 2 * UNITS - DIRECT - 1 + LAGS[-1]:
             send_result(half - DIRECT * width)
             copies.drain("back")
-        for k in todo[:TILES_A_STEP]:
-            grads(k)
-        todo = todo[TILES_A_STEP:]
+        some_grads(2 if t < UNITS + 2 else 1)
 
     copies.drain()
     copies.arrived(("back",), back_in, previous)

time: 178 us -> 178 us (level)
  no operation moved by 1% of the time
where the time goes in v4:
time: 178 us
  Pallas kernels  177 us (99%)
    pallas_call x1, Pallas kernels, tick(): pl.pallas_call(body, out_shape=[pltpu.VMEM((rows, d), bf16), pltpu.VMEM((...  173 us
    pallas_call x1, Pallas kernels, placed(): pl.pallas_call(move, out_shape=[pltpu.HBM(a.shape, a.dtype) for a in arra...  3.91 us

profile of v4, /device:TPU:1, one launch (start us, length us, event | category | flops | bytes accessed | tf_op | source)
XLA Modules:
  0.0 177.9 jit_solution(5592089107220282866)
XLA Ops:
  0.6 173.2 %shard_map.93 = (bf16[16,6144]{1,0:T(8,128)(2,1)S(1)}, bf16[16,6144]{1,0:T(8,128)(2,1)S(1)}, bf16[6144,384]{1,0:T(8,128)(2,1)S(1)}, bf16[384,6144]{1,0:T(8,128)(2,1)S(1)}) custom-call(bf16[16,6144]{1,0:T(8,128)(2,1)} %bitcast.13, bf16[16,6144]{1,0:T(8,128)(2,1)} %bitcast.14, bf16[16,6144]{1,0:T(8,128)(2,1)} %bitcast.15, f32[1,6144]{1,0:T(1,128)} %gain.1, ...), custom_call_target="tpu_custom_call" | custom-call | flops 16911433728 | bytes 37748736 | tf_op jit(solution)/shard_map/pallas_call | solution.py:591
  173.8 3.9 %shard_map.94 = (bf16[16,6144]{1,0:T(8,128)(2,1)}, bf16[16,6144]{1,0:T(8,128)(2,1)}, bf16[6144,384]{1,0:T(8,128)(2,1)}, bf16[384,6144]{1,0:T(8,128)(2,1)}) custom-call(bf16[16,6144]{1,0:T(8,128)(2,1)S(1)} %get-tuple-element.12.refs_0_, bf16[16,6144]{1,0:T(8,128)(2,1)S(1)} %get-tuple-element.13.refs_1_, bf16[6144,384]{1,0:T(8,128)(2,1)S(1)} %get-tuple-element.14.refs_2_, ...), custom_call_target="tpu_custom_call" | custom-call | tf_op jit(solution)/shard_map/pallas_call | solution.py:644
